TPU v7x, 32 devices: a whole 2x2x4 slice. The times are simulated.
32 devices in a mesh: groups: 2 (over y), ctx: 4 (over z), dp: 2 (over x), mp: 2 (over core).
Axes of the slice: x: 2, y: 2, z: 4, core: 2. Of those that a mesh axis runs over, the one named last changes fastest.
Arguments:
- byte_ids: int32 [4, 1024], P(('groups', 'dp'), 'ctx'), parts along dimension 0, may hold values from 0 to 255
- lengths: int32 [4], P(('groups', 'dp')), parts along dimension 0, may hold values from 128 to 1024, as said below
- hidden: bfloat16 [4, 256, 768], P(('groups', 'dp'), 'ctx'), parts along dimension 0
- w_qkv: bfloat16 [768, 3, 768], P(None, None, 'mp'), may hold values from -0.21875 to 0.21875
- w_out: bfloat16 [768, 768], P('mp'), may hold values from -0.21875 to 0.21875
- w_up: bfloat16 [4, 768, 768], P(None, None, 'mp'), may hold values from -0.109375 to 0.109375
- w_head: bfloat16 [768, 256], P('mp'), may hold values from -0.21875 to 0.21875
Outputs:
- grad_hidden: bfloat16 [4, 256, 768], P(('groups', 'dp'), 'ctx'), parts along dimension 0
There are 2 independent parts, one for each index of `groups`. A program takes and returns all parts, laid end to end along the dimension named above; an argument that names none is the same for every part. Nothing has to cross between parts.
Inputs may be any that keep to these rules, and one draw needn't show every extreme that they name: `lengths`: each document's valid byte count; in every draw some document is full, with 1024 valid bytes.
All inputs are finite; a program needn't handle non-finite values.
Results may differ from a plain program's by a relative error of at most 0.025.
Values may be sent and summed in bfloat16 or wider, within the bound.
A program may use at most 64 MiB of HBM per device.

v0:
```python
import jax
import jax.numpy as jnp
from jax import lax
from jax.sharding import PartitionSpec as P

HEAD_DIM = 64


def with_halo(x, sides, width):
    for axis, dim in sides:
        devices, length = (lax.axis_size(axis), x.shape[dim])
        up = [(i, (i + 1) % devices) for i in range(devices - 1)]
        down = [(j, i) for i, j in up]
        last = lax.slice_in_dim(x, length - width, length, axis=dim)
        initial = lax.slice_in_dim(x, 0, width, axis=dim)
        before = lax.ppermute(last, axis, up)
        after = lax.ppermute(initial, axis, down)
        x = jnp.concatenate([before, x, after], axis=dim)
    return x


def pair_sum(values):
    return lax.psum(values, "mp")


def edges(values):
    return with_halo(values, (("ctx", 0),), 1)


def gelu_grad(pre_act, incoming):
    result, pullback = jax.vjp(jax.nn.gelu, pre_act)
    return pullback(incoming)[0]


def body(byte_ids, lengths, hidden, w_qkv, w_out, w_up, w_head):
    inputs = hidden[0]
    rows = inputs.shape[0]
    model_width = inputs.shape[1]
    split_width = w_qkv.shape[2]
    own_heads = split_width // HEAD_DIM
    scaling = HEAD_DIM ** (-0.5)
    length = lengths[0]
    my_first = lax.axis_index("ctx") * rows
    byte_rows = 4 * rows
    flat_qkv = w_qkv.reshape(model_width, 3 * split_width)
    projected = jnp.dot(inputs, flat_qkv, preferred_element_type=jnp.float32).astype(jnp.bfloat16)
    projected = projected.reshape(rows, 3, own_heads, HEAD_DIM)
    queries = projected[:, 0]
    key_rows = projected[:, 1]
    value_rows = projected[:, 2]

    def usable(first_row, count):
        return 4 * (first_row + jnp.arange(count, dtype=jnp.int32)) < length

    running = jnp.full((rows, own_heads), -1e30, jnp.float32)
    key_piece = lax.all_gather(key_rows, "ctx", axis=0, tiled=True)
    value_piece = lax.all_gather(value_rows, "ctx", axis=0, tiled=True)
    keep = usable(jnp.int32(0), key_piece.shape[0])[None, None, :]
    scores = (
        jnp.einsum("qhd,khd->qhk", queries, key_piece, preferred_element_type=jnp.float32) * scaling
    )
    newest = jnp.maximum(running, jnp.max(jnp.where(keep, scores, -1e30), axis=-1))
    weights = jnp.where(keep, jnp.exp(scores - newest[..., None]), 0.0)
    totals = jnp.sum(weights, axis=-1)
    weighted = jnp.einsum(
        "qhk,khd->qhd",
        weights.astype(jnp.bfloat16),
        value_piece,
        preferred_element_type=jnp.float32,
    )
    weighted, running, totals = (weighted, newest, totals)
    attn_heads = (weighted / totals[..., None]).astype(jnp.bfloat16)
    attn = attn_heads.reshape(rows, split_width)
    log_norm = running + jnp.log(totals)
    context = (
        inputs.astype(jnp.float32)
        + pair_sum(jnp.dot(attn, w_out, preferred_element_type=jnp.float32))
    ).astype(jnp.bfloat16)
    extended = edges(context)
    tap_outputs = [
        jnp.dot(extended, w_up[tap], preferred_element_type=jnp.float32) for tap in range(4)
    ]
    phases = []
    for phase in range(4):
        phase_sum = jnp.zeros((rows, split_width), jnp.float32)
        for tap in range(4):
            shifted = 1 + (phase + tap - 1) // 4
            phase_sum = phase_sum + tap_outputs[tap][shifted : shifted + rows]
        phases.append(phase_sum)
    pre_act = jnp.stack(phases, axis=1).reshape(byte_rows, split_width)
    activated = jax.nn.gelu(pre_act).astype(jnp.bfloat16)
    logits = pair_sum(jnp.dot(activated, w_head, preferred_element_type=jnp.float32))
    byte_first = lax.axis_index("ctx") * byte_rows
    byte_mask = byte_first + jnp.arange(byte_rows, dtype=jnp.int32) < length
    inverse = 1.0 / length.astype(jnp.float32)
    softmaxed = jax.nn.softmax(logits, axis=-1)
    onehot = (byte_ids[0][:, None] == jnp.arange(logits.shape[1], dtype=jnp.int32)[None, :]).astype(
        jnp.float32
    )
    logit_grad = ((softmaxed - onehot) * jnp.where(byte_mask, inverse, 0.0)[:, None]).astype(
        jnp.bfloat16
    )
    act_grad = jnp.dot(logit_grad, w_head.T, preferred_element_type=jnp.float32)
    pre_grad = gelu_grad(pre_act, act_grad).astype(jnp.bfloat16)
    grad_ext = edges(pre_grad.reshape(rows, 4 * split_width)).reshape(byte_rows + 8, split_width)
    partial_grad = jnp.zeros((rows, model_width), jnp.float32)
    for offset in range(4):
        window = grad_ext[5 - offset : 5 - offset + byte_rows].astype(jnp.float32)
        tap_sum = jnp.sum(window.reshape(rows, 4, split_width), axis=1).astype(jnp.bfloat16)
        partial_grad = partial_grad + jnp.dot(
            tap_sum, w_up[offset].T, preferred_element_type=jnp.float32
        )
    context_grad = pair_sum(partial_grad)
    attn_grad = jnp.dot(
        context_grad.astype(jnp.bfloat16), w_out.T, preferred_element_type=jnp.float32
    ).astype(jnp.bfloat16)
    attn_grad = attn_grad.reshape(rows, own_heads, HEAD_DIM)
    row_dots = jnp.sum(attn_grad.astype(jnp.float32) * attn_heads.astype(jnp.float32), axis=-1)
    key_piece = lax.all_gather(key_rows, "ctx", axis=0, tiled=True)
    value_piece = lax.all_gather(value_rows, "ctx", axis=0, tiled=True)
    keep = usable(jnp.int32(0), key_piece.shape[0])[None, None, :]
    scores = (
        jnp.einsum("qhd,khd->qhk", queries, key_piece, preferred_element_type=jnp.float32) * scaling
    )
    probs = jnp.where(keep, jnp.exp(scores - log_norm[..., None]), 0.0)
    product = jnp.einsum("qhd,khd->qhk", attn_grad, value_piece, preferred_element_type=jnp.float32)
    score_grad = (probs * (product - row_dots[..., None])).astype(jnp.bfloat16)
    query_sum = jnp.einsum(
        "qhk,khd->qhd", score_grad, key_piece, preferred_element_type=jnp.float32
    )
    query_grad = (query_sum * scaling).astype(jnp.bfloat16)
    key_keep = usable(my_first, rows)[None, None, :]
    norm_all, dots_all = (
        lax.all_gather(log_norm, "ctx", axis=0, tiled=True),
        lax.all_gather(row_dots, "ctx", axis=0, tiled=True),
    )
    query_piece = lax.all_gather(queries, "ctx", axis=0, tiled=True)
    outgrad_piece = lax.all_gather(attn_grad, "ctx", axis=0, tiled=True)
    count = query_piece.shape[0]
    scores = (
        jnp.einsum("qhd,khd->qhk", query_piece, key_rows, preferred_element_type=jnp.float32)
        * scaling
    )
    probs = jnp.where(key_keep, jnp.exp(scores - norm_all[..., None]), 0.0)
    product = jnp.einsum(
        "qhd,khd->qhk", outgrad_piece, value_rows, preferred_element_type=jnp.float32
    )
    score_grad = (probs * (product - dots_all[..., None])).astype(jnp.bfloat16)
    key_sum = jnp.einsum(
        "qhk,qhd->khd", score_grad, query_piece, preferred_element_type=jnp.float32
    )
    value_sum = jnp.einsum(
        "qhk,qhd->khd",
        probs.astype(jnp.bfloat16),
        outgrad_piece,
        preferred_element_type=jnp.float32,
    )
    key_sum, value_sum = (key_sum, value_sum)
    key_grad = (key_sum * scaling).astype(jnp.bfloat16)
    value_grad = value_sum.astype(jnp.bfloat16)
    stacked = jnp.stack([query_grad, key_grad, value_grad], axis=1).reshape(rows, 3 * split_width)
    back_proj = pair_sum(jnp.dot(stacked, flat_qkv.T, preferred_element_type=jnp.float32))
    input_grad = (context_grad + back_proj).astype(jnp.bfloat16)
    return input_grad[None]


def solution(mesh):
    placed = (
        P(("groups", "dp"), "ctx"),
        P(("groups", "dp")),
        P(("groups", "dp"), "ctx", None),
        P(None, None, "mp"),
        P("mp", None),
        P(None, None, "mp"),
        P("mp", None),
    )
    return jax.shard_map(
        body,
        mesh=mesh,
        in_specs=placed,
        out_specs=P(("groups", "dp"), "ctx", None),
        check_vma=False,
    )
```

profile of v0, /device:TPU:0, one launch (start us, length us, event | category | flops | bytes accessed | tf_op | source)
XLA Modules:
  0.0 255.1 jit_solution(12642925866357019696)
XLA Ops:
  7.3 2.6 %copy.24 = bf16[768,3,384]{0,2,1:T(8,128)(2,1)S(1)} copy(bf16[768,3,384]{2,0,1:T(8,128)(2,1)} %param.10) | data formatting | bytes 3538944 | tf_op args[3]
  12.2 17.3 %all-gather.1 = bf16[256,1,6,64]{3,2,1,0:T(8,128)(2,1)S(1)} all-gather(bf16[64,1,6,64]{3,2,1,0:T(8,128)(2,1)S(1)} %get-tuple-element.11), channel_id=3, replica_groups=mesh['groups'=2,'ctx'=4,'dp'=2,'mp'=2] {'ctx'}, dimensions={0}, use_global_device_ids=true | all-gather | bytes 245760 | tf_op jit(solution)/shard_map/all_gather | solution.py:56
  29.6 1.0 copy.30
  31.4 1.2 select_reduce_fusion
  32.7 16.3 %all-gather = bf16[256,1,6,64]{3,2,1,0:T(8,128)(2,1)S(1)} all-gather(bf16[64,1,6,64]{3,2,1,0:T(8,128)(2,1)S(1)} %get-tuple-element.9), channel_id=2, replica_groups=mesh['groups'=2,'ctx'=4,'dp'=2,'mp'=2] {'ctx'}, dimensions={0}, use_global_device_ids=true | all-gather | bytes 245760 | tf_op jit(solution)/shard_map/all_gather | solution.py:57
  49.0 1.0 copy.27
  50.2 1.2 fusion.12
  52.5 18.5 %all-reduce.5.cloned.1.call-done = f32[64,768]{1,0:T(8,128)} async-done(((f32[64,768]{1,0:T(8,128)}), f32[64,768]{1,0:T(8,128)}) %all-reduce.5.cloned.1.call-update) | async-done | bytes 196624 | tf_op jit(solution)/shard_map/psum | solution.py:23
  72.0 3.6 %collective-permute-start = (bf16[1,768]{1,0:T(2,128)(2,1)S(1)}, bf16[1,768]{1,0:T(2,128)(2,1)S(1)}, u32[]{:S(2)}, u32[]{:S(2)}) collective-permute-start(bf16[1,768]{1,0:T(2,128)(2,1)S(1)} %get-tuple-element.17), channel_id=1, source_target_pairs={{0,4},{4,8},{8,12},{1,5},{5,9},{9,13},{2,6},{6,10},{10,14},{3,7},{... | collective-permute-start | bytes 4616 | tf_op jit(solution)/shard_map/ppermute | solution.py:16
  75.6 1.3 collective-permute-start.1
  77.0 4.2 %collective-permute-done.1 = bf16[1,768]{1,0:T(2,128)(2,1)S(1)} collective-permute-done((bf16[1,768]{1,0:T(2,128)(2,1)S(1)}, bf16[1,768]{1,0:T(2,128)(2,1)S(1)}, u32[]{:S(2)}, u32[]{:S(2)}) %collective-permute-start.1) | collective-permute-done | bytes 1568 | tf_op jit(solution)/shard_map/ppermute | solution.py:17
  81.1 1.3 fusion.22
  82.4 1.3 fusion.19
  83.8 1.3 fusion.29
  85.1 1.3 fusion.85
  87.6 2.0 fusion.67
  90.2 17.8 %all-reduce.7.cloned.1.call-done = f32[256,256]{1,0:T(8,128)} async-done(((f32[256,256]{1,0:T(8,128)}), f32[256,256]{1,0:T(8,128)}) %all-reduce.7.cloned.1.call-update) | async-done | bytes 262160 | tf_op jit(solution)/shard_map/psum | solution.py:23
  108.0 1.1 reduce_max.19
  109.1 1.1 fusion.53
  110.2 1.6 fusion.45
  111.9 4.2 %collective-permute-start.2 = (bf16[1,1536]{1,0:T(2,128)(2,1)S(1)}, bf16[1,1536]{1,0:T(2,128)(2,1)}, u32[]{:S(2)}, u32[]{:S(2)}) collective-permute-start(bf16[1,1536]{1,0:T(2,128)(2,1)S(1)} %bitcast.170), channel_id=1, source_target_pairs={{0,4},{4,8},{8,12},{1,5},{5,9},{9,13},{2,6},{6,10},{10,14},{3,7},{... | collective-permute-start | bytes 9224 | tf_op jit(solution)/shard_map/ppermute | solution.py:16
  116.8 1.3 collective-permute-start.3
  118.0 15.7 %all-gather.2 = bf16[256,1,6,64]{3,0,2,1:T(8,128)(2,1)S(1)} all-gather(bf16[64,1,6,64]{3,0,2,1:T(8,128)(2,1)S(1)} %copy.46), channel_id=4, replica_groups=mesh['groups'=2,'ctx'=4,'dp'=2,'mp'=2] {'ctx'}, dimensions={0}, use_global_device_ids=true | all-gather | bytes 245760 | tf_op jit(solution)/shard_map/all_gather | solution.py:137
  133.7 13.4 %all-gather.3 = f32[4,64,6]{1,2,0:T(8,128)S(1)} all-gather(f32[1,64,6]{1,2,0:T(8,128)S(1)} %bitcast.168), channel_id=1, replica_groups=mesh['groups'=2,'ctx'=4,'dp'=2,'mp'=2] {'ctx'}, dimensions={0}, use_global_device_ids=true | all-gather | bytes 7680 | tf_op jit(solution)/shard_map/all_gather | solution.py:134
  148.1 1.8 reduce_sum.69
  149.8 1.4 pad_maximum_fusion.2
  151.3 1.1 reshape.86
  153.2 1.0 reshape.87
  155.1 2.1 fusion.27
  157.1 1.0 reshape.89
  159.3 1.4 convolution_add_fusion.2
  160.7 1.4 convolution_add_fusion.1
  162.2 2.1 convolution_add_fusion
  164.3 1.2 fusion.8
  165.5 18.4 %all-reduce.9.cloned.1.call-done = f32[64,768]{1,0:T(8,128)} async-done(((f32[64,768]{1,0:T(8,128)}), f32[64,768]{1,0:T(8,128)}) %all-reduce.9.cloned.1.call-update) | async-done | bytes 196624 | tf_op jit(solution)/shard_map/psum | solution.py:23
  183.9 1.9 convolution_convert_fusion.2
  185.7 1.5 copy.33
  187.3 1.0 multiply_reduce_fusion
  188.2 1.7 copy.37
  189.9 2.1 fusion.16
  192.0 13.4 %all-gather.4 = f32[4,64,6]{1,2,0:T(8,128)S(1)} all-gather(f32[1,64,6]{1,2,0:T(8,128)S(1)} %bitcast.169), channel_id=1, replica_groups=mesh['groups'=2,'ctx'=4,'dp'=2,'mp'=2] {'ctx'}, dimensions={0}, use_global_device_ids=true | all-gather | bytes 7680 | tf_op jit(solution)/shard_map/all_gather | solution.py:135
  205.5 17.8 %all_gather.24 = bf16[256,6,64]{2,1,0:T(8,128)(2,1)} all-gather(bf16[64,6,64]{2,1,0:T(8,128)(2,1)} %copy.37), channel_id=1, replica_groups=mesh['groups'=2,'ctx'=4,'dp'=2,'mp'=2] {'ctx'}, dimensions={0}, use_global_device_ids=true | all-gather | bytes 245760 | tf_op jit(solution)/shard_map/all_gather | solution.py:138
  223.3 1.3 copy.41
  225.5 1.3 fusion.15
  226.7 1.0 pad_maximum_fusion.1
  227.7 1.2 fusion.104
  228.9 18.0 %all-reduce.11.cloned.1.call-done = f32[64,768]{1,0:T(8,128)} async-done(((f32[64,768]{1,0:T(8,128)}), f32[64,768]{1,0:T(8,128)}) %all-reduce.11.cloned.1.call-update) | async-done | bytes 196624 | tf_op jit(solution)/shard_map/psum | solution.py:23
  246.9 1.7 fusion.75
  (62 shorter events, 12.6 us)
Async XLA Ops:
  6.5 44.9 %copy-start = (bf16[384,768]{1,0:T(8,128)(2,1)S(1)}, bf16[384,768]{1,0:T(8,128)(2,1)}, u32[]{:S(2)}) copy-start(bf16[384,768]{1,0:T(8,128)(2,1)} %param.11) | copy-start | bytes 1769476
  6.5 3.4 %copy-start.3 = (bf16[1,64,768]{2,1,0:T(8,128)(2,1)S(1)}, bf16[1,64,768]{2,1,0:T(8,128)(2,1)}, u32[]{:S(2)}) copy-start(bf16[1,64,768]{2,1,0:T(8,128)(2,1)} %param.9) | copy-start | bytes 294916
  6.5 64.5 %all-reduce.5.cloned.1.call-start = ((), (), s32[]{:S(2)}) async-start(), calls=%async_computation | async-start | bytes 393216 | tf_op jit(solution)/shard_map/psum | solution.py:23
  7.3 42.9 %copy-start.8 = (pred[256]{0:T(512)(128)(4,1)}, pred[256]{0:T(512)(128)(4,1)S(1)}, u32[]{:S(2)}) copy-start(pred[256]{0:T(512)(128)(4,1)S(1)} %multiply_compare_fusion) | copy-start | bytes 772
  11.6 0.7 copy-start.2
  11.6 39.8 %copy-start.1 = (bf16[64,1,6,64]{3,2,1,0:T(8,128)(2,1)}, bf16[64,1,6,64]{3,2,1,0:T(8,128)(2,1)S(1)}, u32[]{:S(2)}) copy-start(bf16[64,1,6,64]{3,2,1,0:T(8,128)(2,1)S(1)} %get-tuple-element.9) | copy-start | bytes 147460
  49.9 21.1 %copy-start.4 = (bf16[1,64,768]{2,1,0:T(8,128)(2,1)S(1)}, bf16[1,64,768]{2,1,0:T(8,128)(2,1)}, u32[]{:S(2)}) copy-start(bf16[1,64,768]{2,1,0:T(8,128)(2,1)} %param.9) | copy-start | bytes 294916
  51.4 35.0 %copy-start.5 = (bf16[64,6,64]{0,2,1:T(8,128)(2,1)}, bf16[64,6,64]{0,2,1:T(8,128)(2,1)S(1)}, u32[]{:S(2)}) copy-start(bf16[64,6,64]{0,2,1:T(8,128)(2,1)S(1)} %fusion.12) | copy-start | bytes 147460
  52.4 55.6 %all-reduce.7.cloned.1.call-start = ((), (), s32[]{:S(2)}) async-start(), calls=%async_computation.1 | async-start | bytes 524288 | tf_op jit(solution)/shard_map/psum | solution.py:23
  72.0 5.0 %collective-permute-start = (bf16[1,768]{1,0:T(2,128)(2,1)S(1)}, bf16[1,768]{1,0:T(2,128)(2,1)S(1)}, u32[]{:S(2)}, u32[]{:S(2)}) collective-permute-start(bf16[1,768]{1,0:T(2,128)(2,1)S(1)} %get-tuple-element.17), channel_id=1, source_target_pairs={{0,4},{4,8},{8,12},{1,5},{5,9},{9,13},{2,6},{6,10},{10,14},{3,7},{... | collective-permute-start | bytes 4616 | tf_op jit(solution)/shard_map/ppermute | solution.py:16
  75.6 5.5 %collective-permute-start.1 = (bf16[1,768]{1,0:T(2,128)(2,1)S(1)}, bf16[1,768]{1,0:T(2,128)(2,1)S(1)}, u32[]{:S(2)}, u32[]{:S(2)}) collective-permute-start(bf16[1,768]{1,0:T(2,128)(2,1)S(1)} %get-tuple-element.18), channel_id=1, source_target_pairs={{4,0},{8,4},{12,8},{5,1},{9,5},{13,9},{6,2},{10,6},{14,10},{7,3},{... | collective-permute-start | bytes 4616 | tf_op jit(solution)/shard_map/ppermute | solution.py:17
  86.4 23.8 %copy-start.9 = (s32[1,256]{1,0:T(1,128)S(1)}, s32[1,256]{1,0:T(1,128)}, u32[]{:S(2)}) copy-start(s32[1,256]{1,0:T(1,128)} %param.7) | copy-start | bytes 3076
  89.6 94.2 %all-reduce.9.cloned.1.call-start = ((), (), s32[]{:S(2)}) async-start(), calls=%async_computation.2 | async-start | bytes 393216 | tf_op jit(solution)/shard_map/psum | solution.py:23
  90.2 43.5 %copy-start.6 = (f32[64,6]{0,1:T(8,128)}, f32[64,6]{0,1:T(8,128)S(1)}, u32[]{:S(2)}) copy-start(f32[64,6]{0,1:T(8,128)S(1)} %log_add_fusion) | copy-start | bytes 4612
  111.9 37.9 %collective-permute-start.2 = (bf16[1,1536]{1,0:T(2,128)(2,1)S(1)}, bf16[1,1536]{1,0:T(2,128)(2,1)}, u32[]{:S(2)}, u32[]{:S(2)}) collective-permute-start(bf16[1,1536]{1,0:T(2,128)(2,1)S(1)} %bitcast.170), channel_id=1, source_target_pairs={{0,4},{4,8},{8,12},{1,5},{5,9},{9,13},{2,6},{6,10},{10,14},{3,7},{... | collective-permute-start | bytes 9224 | tf_op jit(solution)/shard_map/ppermute | solution.py:16
  116.8 33.1 %collective-permute-start.3 = (bf16[1,1536]{1,0:T(2,128)(2,1)}, bf16[1,1536]{1,0:T(2,128)(2,1)}, u32[]{:S(2)}, u32[]{:S(2)}) collective-permute-start(bf16[1,1536]{1,0:T(2,128)(2,1)} %bitcast.43), channel_id=1, source_target_pairs={{4,0},{8,4},{12,8},{5,1},{9,5},{13,9},{6,2},{10,6},{14,10},{7,3},{... | collective-permute-start | bytes 9224 | tf_op jit(solution)/shard_map/ppermute | solution.py:17
  160.7 29.2 %copy-start.7 = (f32[64,6]{0,1:T(8,128)S(1)}, f32[64,6]{0,1:T(8,128)}, u32[]{:S(2)}) copy-start(f32[64,6]{0,1:T(8,128)} %copy-done.6) | copy-start | bytes 4612
  164.2 82.7 %all-reduce.11.cloned.1.call-start = ((), (), s32[]{:S(2)}) async-start(), calls=%async_computation.3 | async-start | bytes 393216 | tf_op jit(solution)/shard_map/psum | solution.py:23
Sparse Core Ops, SparseCore 0:
  52.5 18.4 all-reduce.4
  89.8 18.2 all-reduce.6
  164.4 19.4 all-reduce.8
  229.0 17.8 all-reduce.10
where the time goes:
time: 256 us; the launch traced here: 255 us
  blocking collectives  93.9 us (37%)
  waiting for transfers between devices  77 us (30%)
  matrix products  28.3 us (11%)
  local copies, waits for them, and re-layouts  18.3 us (7%)
  between operations  14.2 us (6%)
  other arithmetic  12.9 us (5%)
  starting transfers between devices  10.6 us (4%)
    psum x4, waiting for transfers between devices, pair_sum(): return lax.psum(values, 'mp')  72.7 us
    all_gather x1, blocking collectives, body(): outgrad_piece = lax.all_gather(attn_grad, 'ctx', axis=0, tiled=True)  17.8 us
    all_gather x1, blocking collectives, body(): key_piece = lax.all_gather(key_rows, 'ctx', axis=0, tiled=True)  17.3 us
    all_gather x1, blocking collectives, body(): value_piece = lax.all_gather(value_rows, 'ctx', axis=0, tiled=True)  16.3 us
    all_gather x1, blocking collectives, body(): query_piece = lax.all_gather(queries, 'ctx', axis=0, tiled=True)  15.7 us
    all_gather x1, blocking collectives, body(): lax.all_gather(row_dots, 'ctx', axis=0, tiled=True)  13.4 us
    all_gather x1, blocking collectives, body(): lax.all_gather(log_norm, 'ctx', axis=0, tiled=True)  13.4 us
    ppermute x2, starting transfers between devices, with_halo(): before = lax.ppermute(last, axis, up)  7.88 us
  transfers between devices with their start and end apart: 8, of which 5 were waited for; matrix products, arithmetic and copies ran while one was open for 2% of the time, Pallas kernels for 0%

commit v1 on v0

--- a/solution.py
+++ b/solution.py
@@ -4,6 +4,19 @@
 from jax.sharding import PartitionSpec as P
 
 HEAD_DIM = 64
+
+
+def ring_gather(x, axis, dim):
+    length, index, rows = (lax.axis_size(axis), lax.axis_index(axis), x.shape[dim])
+    right = [(i, (i + 1) % length) for i in range(length)]
+    out = jnp.zeros((*x.shape[:dim], length * rows, *x.shape[dim + 1 :]), x.dtype)
+    current = x
+    for step in range(length):
+        owner = (index - step) % length
+        out = lax.dynamic_update_slice_in_dim(out, current, owner * rows, axis=dim)
+        if step < length - 1:
+            current = lax.ppermute(current, axis, right)
+    return out
 
 
 def with_halo(x, sides, width):
@@ -132,7 +145,7 @@
     key_keep = usable(my_first, rows)[None, None, :]
     norm_all, dots_all = (
         lax.all_gather(log_norm, "ctx", axis=0, tiled=True),
-        lax.all_gather(row_dots, "ctx", axis=0, tiled=True),
+        ring_gather(row_dots, "ctx", 0),
     )
     query_piece = lax.all_gather(queries, "ctx", axis=0, tiled=True)
     outgrad_piece = lax.all_gather(attn_grad, "ctx", axis=0, tiled=True)

time: 256 us -> 233 us (0.910)
  blocking collectives: 93.9 us -> 78.5 us
  waiting for transfers between devices: 77 us -> 64.6 us
  starting transfers between devices: 10.6 us -> 14.7 us
    psum x4, waiting for transfers between devices: 72.7 us -> 57.2 us  [pair_sum(): return lax.psum(values, 'mp')]
    all_gather x1 -> x0, blocking collectives: 13.4 us -> none  [body(): lax.all_gather(row_dots, 'ctx', axis=0, tiled=True)]
    ppermute x0 -> x3, starting transfers between devices: none -> 4.12 us  [ring_gather(): current = lax.ppermute(current, axis, right)]
    ppermute x0 -> x3, waiting for transfers between devices: none -> 3.26 us  [ring_gather(): current = lax.ppermute(current, axis, right)]
  transfers between devices with their start and end apart: 8 -> 11, of which waited for: 5 -> 7; matrix products, arithmetic and copies ran while one was open for 2% -> 5% of each run, Pallas kernels for 0% -> 0%
where the time goes in v1:
time: 233 us; the launch traced here: 231 us
  blocking collectives  78.5 us (34%)
  waiting for transfers between devices  64.6 us (28%)
  matrix products  28 us (12%)
  local copies, waits for them, and re-layouts  18.3 us (8%)
  starting transfers between devices  14.7 us (6%)
  between operations  14.4 us (6%)
  other arithmetic  12.8 us (5%)
    psum x4, waiting for transfers between devices, pair_sum(): return lax.psum(values, 'mp')  57.2 us
    all_gather x1, blocking collectives, body(): key_piece = lax.all_gather(key_rows, 'ctx', axis=0, tiled=True)  17.3 us
    all_gather x1, blocking collectives, body(): value_piece = lax.all_gather(value_rows, 'ctx', axis=0, tiled=True)  16.3 us
    all_gather x1, blocking collectives, body(): outgrad_piece = lax.all_gather(attn_grad, 'ctx', axis=0, tiled=True)  15.8 us
    all_gather x1, blocking collectives, body(): query_piece = lax.all_gather(queries, 'ctx', axis=0, tiled=True)  15.3 us
    all_gather x1, blocking collectives, body(): lax.all_gather(log_norm, 'ctx', axis=0, tiled=True)  13.8 us
    ppermute x2, starting transfers between devices, with_halo(): before = lax.ppermute(last, axis, up)  7.88 us
    dot_general x4, matrix products, body(): jnp.dot(tap_sum, w_up[offset].T, preferred_element_type=jnp.float32)  6.98 us
  transfers between devices with their start and end apart: 11, of which 7 were waited for; matrix products, arithmetic and copies ran while one was open for 5% of the time, Pallas kernels for 0%

profile of v1, /device:TPU:0, one launch (start us, length us, event | category | flops | bytes accessed | tf_op | source)
XLA Modules:
  0.0 231.3 jit_solution(7659285613616905063)
XLA Ops:
  7.3 2.6 %copy.24 = bf16[768,3,384]{0,2,1:T(8,128)(2,1)S(1)} copy(bf16[768,3,384]{2,0,1:T(8,128)(2,1)} %param.10) | data formatting | bytes 3538944 | tf_op args[3]
  12.2 17.3 %all-gather.1 = bf16[256,1,6,64]{3,2,1,0:T(8,128)(2,1)S(1)} all-gather(bf16[64,1,6,64]{3,2,1,0:T(8,128)(2,1)S(1)} %get-tuple-element.11), channel_id=3, replica_groups=mesh['groups'=2,'ctx'=4,'dp'=2,'mp'=2] {'ctx'}, dimensions={0}, use_global_device_ids=true | all-gather | bytes 245760 | tf_op jit(solution)/shard_map/all_gather | solution.py:69
  31.4 1.2 select_reduce_fusion
  32.7 16.3 %all-gather = bf16[256,1,6,64]{3,2,1,0:T(8,128)(2,1)S(1)} all-gather(bf16[64,1,6,64]{3,2,1,0:T(8,128)(2,1)S(1)} %get-tuple-element.9), channel_id=2, replica_groups=mesh['groups'=2,'ctx'=4,'dp'=2,'mp'=2] {'ctx'}, dimensions={0}, use_global_device_ids=true | all-gather | bytes 245760 | tf_op jit(solution)/shard_map/all_gather | solution.py:70
  50.2 1.2 fusion.9
  53.1 18.0 %all-reduce.5.cloned.1.call-done = f32[64,768]{1,0:T(8,128)} async-done(((f32[64,768]{1,0:T(8,128)}), f32[64,768]{1,0:T(8,128)}) %all-reduce.5.cloned.1.call-update) | async-done | bytes 196624 | tf_op jit(solution)/shard_map/psum | solution.py:36
  72.0 3.6 %collective-permute-start = (bf16[1,768]{1,0:T(2,128)(2,1)S(1)}, bf16[1,768]{1,0:T(2,128)(2,1)S(1)}, u32[]{:S(2)}, u32[]{:S(2)}) collective-permute-start(bf16[1,768]{1,0:T(2,128)(2,1)S(1)} %get-tuple-element.17), channel_id=1, source_target_pairs={{0,4},{4,8},{8,12},{1,5},{5,9},{9,13},{2,6},{6,10},{10,14},{3,7},{... | collective-permute-start | bytes 4616 | tf_op jit(solution)/shard_map/ppermute | solution.py:29
  75.6 1.3 collective-permute-start.1
  77.0 4.1 %collective-permute-done.1 = bf16[1,768]{1,0:T(2,128)(2,1)S(1)} collective-permute-done((bf16[1,768]{1,0:T(2,128)(2,1)S(1)}, bf16[1,768]{1,0:T(2,128)(2,1)S(1)}, u32[]{:S(2)}, u32[]{:S(2)}) %collective-permute-start.1) | collective-permute-done | bytes 1568 | tf_op jit(solution)/shard_map/ppermute | solution.py:30
  81.1 1.3 fusion.19
  82.4 1.3 fusion.16
  83.8 1.3 fusion.26
  85.1 1.3 fusion.82
  87.6 2.0 fusion.64
  89.7 15.3 %all-gather.2 = bf16[256,1,6,64]{3,0,2,1:T(8,128)(2,1)S(1)} all-gather(bf16[64,1,6,64]{3,0,2,1:T(8,128)(2,1)S(1)} %copy.45), channel_id=4, replica_groups=mesh['groups'=2,'ctx'=4,'dp'=2,'mp'=2] {'ctx'}, dimensions={0}, use_global_device_ids=true | all-gather | bytes 245760 | tf_op jit(solution)/shard_map/all_gather | solution.py:150
  105.0 3.1 %all-reduce.7.cloned.1.call-done = f32[256,256]{1,0:T(8,128)} async-done(((f32[256,256]{1,0:T(8,128)}), f32[256,256]{1,0:T(8,128)}) %all-reduce.7.cloned.1.call-update) | async-done | bytes 262160 | tf_op jit(solution)/shard_map/psum | solution.py:36
  108.0 1.1 reduce_max.19
  109.1 1.1 fusion.50
  110.2 1.6 fusion.42
  111.9 4.2 %collective-permute-start.2 = (bf16[1,1536]{1,0:T(2,128)(2,1)S(1)}, bf16[1,1536]{1,0:T(2,128)(2,1)}, u32[]{:S(2)}, u32[]{:S(2)}) collective-permute-start(bf16[1,1536]{1,0:T(2,128)(2,1)S(1)} %bitcast.158), channel_id=1, source_target_pairs={{0,4},{4,8},{8,12},{1,5},{5,9},{9,13},{2,6},{6,10},{10,14},{3,7},{... | collective-permute-start | bytes 9224 | tf_op jit(solution)/shard_map/ppermute | solution.py:29
  116.8 1.3 collective-permute-start.3
  118.1 13.8 %all-gather.3 = f32[4,64,6]{1,2,0:T(8,128)S(1)} all-gather(f32[1,64,6]{1,2,0:T(8,128)S(1)} %bitcast.157), channel_id=1, replica_groups=mesh['groups'=2,'ctx'=4,'dp'=2,'mp'=2] {'ctx'}, dimensions={0}, use_global_device_ids=true | all-gather | bytes 7680 | tf_op jit(solution)/shard_map/all_gather | solution.py:147
  132.8 1.8 reduce_sum.69
  134.6 1.4 pad_maximum_fusion.2
  136.0 1.1 reshape.105
  137.9 1.0 reshape.106
  139.8 2.1 fusion.24
  141.9 1.0 reshape.108
  144.0 1.4 convolution_add_fusion.2
  145.5 1.4 convolution_add_fusion.1
  146.9 2.1 convolution_add_fusion
  149.0 1.2 fusion.6
  150.2 18.4 %all-reduce.9.cloned.1.call-done = f32[64,768]{1,0:T(8,128)} async-done(((f32[64,768]{1,0:T(8,128)}), f32[64,768]{1,0:T(8,128)}) %all-reduce.9.cloned.1.call-update) | async-done | bytes 196624 | tf_op jit(solution)/shard_map/psum | solution.py:36
  168.6 1.9 convolution_convert_fusion.2
  170.4 1.5 copy.33
  172.0 1.0 multiply_reduce_fusion
  173.0 1.8 collective-permute-start.4
  174.8 2.1 fusion.12
  176.9 1.1 copy.37
  178.4 1.1 collective-permute-start.5
  179.5 15.8 %all_gather.21 = bf16[256,6,64]{2,1,0:T(8,128)(2,1)} all-gather(bf16[64,6,64]{2,1,0:T(8,128)(2,1)S(1)} %copy.37), channel_id=1, replica_groups=mesh['groups'=2,'ctx'=4,'dp'=2,'mp'=2] {'ctx'}, dimensions={0}, use_global_device_ids=true | all-gather | bytes 245760 | tf_op jit(solution)/shard_map/all_gather | solution.py:151
  195.3 1.3 copy.40
  196.6 1.3 collective-permute-start.6
  199.3 2.8 %collective-permute-done.6 = f32[64,6]{0,1:T(8,128)S(1)} collective-permute-done((f32[64,6]{0,1:T(8,128)S(1)}, f32[64,6]{0,1:T(8,128)S(1)}, u32[]{:S(2)}, u32[]{:S(2)}) %collective-permute-start.6) | collective-permute-done | bytes 1568 | tf_op jit(solution)/shard_map/ppermute | solution.py:18
  203.2 1.1 pad_maximum_fusion.1
  204.3 1.2 fusion.101
  205.5 17.8 %all-reduce.11.cloned.1.call-done = f32[64,768]{1,0:T(8,128)} async-done(((f32[64,768]{1,0:T(8,128)}), f32[64,768]{1,0:T(8,128)}) %all-reduce.11.cloned.1.call-update) | async-done | bytes 196624 | tf_op jit(solution)/shard_map/psum | solution.py:36
  223.2 1.6 fusion.72
  (74 shorter events, 16.6 us)
Async XLA Ops:
  6.5 44.9 %copy-start = (bf16[384,768]{1,0:T(8,128)(2,1)S(1)}, bf16[384,768]{1,0:T(8,128)(2,1)}, u32[]{:S(2)}) copy-start(bf16[384,768]{1,0:T(8,128)(2,1)} %param.11) | copy-start | bytes 1769476
  6.5 3.4 %copy-start.5 = (bf16[1,64,768]{2,1,0:T(8,128)(2,1)S(1)}, bf16[1,64,768]{2,1,0:T(8,128)(2,1)}, u32[]{:S(2)}) copy-start(bf16[1,64,768]{2,1,0:T(8,128)(2,1)} %param.9) | copy-start | bytes 294916
  6.5 64.5 %all-reduce.5.cloned.1.call-start = ((), (), s32[]{:S(2)}) async-start(), calls=%async_computation | async-start | bytes 393216 | tf_op jit(solution)/shard_map/psum | solution.py:36
  7.3 42.9 %copy-start.10 = (pred[256]{0:T(512)(128)(4,1)}, pred[256]{0:T(512)(128)(4,1)S(1)}, u32[]{:S(2)}) copy-start(pred[256]{0:T(512)(128)(4,1)S(1)} %multiply_compare_fusion) | copy-start | bytes 772
  11.6 0.7 copy-start.3
  11.6 39.8 %copy-start.1 = (bf16[64,1,6,64]{3,2,1,0:T(8,128)(2,1)}, bf16[64,1,6,64]{3,2,1,0:T(8,128)(2,1)S(1)}, u32[]{:S(2)}) copy-start(bf16[64,1,6,64]{3,2,1,0:T(8,128)(2,1)S(1)} %get-tuple-element.9) | copy-start | bytes 147460
  49.9 21.1 %copy-start.6 = (bf16[1,64,768]{2,1,0:T(8,128)(2,1)S(1)}, bf16[1,64,768]{2,1,0:T(8,128)(2,1)}, u32[]{:S(2)}) copy-start(bf16[1,64,768]{2,1,0:T(8,128)(2,1)} %param.9) | copy-start | bytes 294916
  51.4 35.0 %copy-start.7 = (bf16[64,6,64]{0,2,1:T(8,128)(2,1)}, bf16[64,6,64]{0,2,1:T(8,128)(2,1)S(1)}, u32[]{:S(2)}) copy-start(bf16[64,6,64]{0,2,1:T(8,128)(2,1)S(1)} %fusion.9) | copy-start | bytes 147460
  52.4 55.6 %all-reduce.7.cloned.1.call-start = ((), (), s32[]{:S(2)}) async-start(), calls=%async_computation.1 | async-start | bytes 524288 | tf_op jit(solution)/shard_map/psum | solution.py:36
  72.0 5.0 %collective-permute-start = (bf16[1,768]{1,0:T(2,128)(2,1)S(1)}, bf16[1,768]{1,0:T(2,128)(2,1)S(1)}, u32[]{:S(2)}, u32[]{:S(2)}) collective-permute-start(bf16[1,768]{1,0:T(2,128)(2,1)S(1)} %get-tuple-element.17), channel_id=1, source_target_pairs={{0,4},{4,8},{8,12},{1,5},{5,9},{9,13},{2,6},{6,10},{10,14},{3,7},{... | collective-permute-start | bytes 4616 | tf_op jit(solution)/shard_map/ppermute | solution.py:29
  75.6 5.5 %collective-permute-start.1 = (bf16[1,768]{1,0:T(2,128)(2,1)S(1)}, bf16[1,768]{1,0:T(2,128)(2,1)S(1)}, u32[]{:S(2)}, u32[]{:S(2)}) collective-permute-start(bf16[1,768]{1,0:T(2,128)(2,1)S(1)} %get-tuple-element.18), channel_id=1, source_target_pairs={{4,0},{8,4},{12,8},{5,1},{9,5},{13,9},{6,2},{10,6},{14,10},{7,3},{... | collective-permute-start | bytes 4616 | tf_op jit(solution)/shard_map/ppermute | solution.py:30
  86.4 23.8 %copy-start.11 = (s32[1,256]{1,0:T(1,128)S(1)}, s32[1,256]{1,0:T(1,128)}, u32[]{:S(2)}) copy-start(s32[1,256]{1,0:T(1,128)} %param.7) | copy-start | bytes 3076
  89.6 78.9 %all-reduce.9.cloned.1.call-start = ((), (), s32[]{:S(2)}) async-start(), calls=%async_computation.2 | async-start | bytes 393216 | tf_op jit(solution)/shard_map/psum | solution.py:36
  105.0 13.1 %copy-start.8 = (f32[64,6]{0,1:T(8,128)}, f32[64,6]{0,1:T(8,128)S(1)}, u32[]{:S(2)}) copy-start(f32[64,6]{0,1:T(8,128)S(1)} %log_add_fusion) | copy-start | bytes 4612
  111.9 22.7 %collective-permute-start.2 = (bf16[1,1536]{1,0:T(2,128)(2,1)S(1)}, bf16[1,1536]{1,0:T(2,128)(2,1)}, u32[]{:S(2)}, u32[]{:S(2)}) collective-permute-start(bf16[1,1536]{1,0:T(2,128)(2,1)S(1)} %bitcast.158), channel_id=1, source_target_pairs={{0,4},{4,8},{8,12},{1,5},{5,9},{9,13},{2,6},{6,10},{10,14},{3,7},{... | collective-permute-start | bytes 9224 | tf_op jit(solution)/shard_map/ppermute | solution.py:29
  116.8 17.8 %collective-permute-start.3 = (bf16[1,1536]{1,0:T(2,128)(2,1)}, bf16[1,1536]{1,0:T(2,128)(2,1)}, u32[]{:S(2)}, u32[]{:S(2)}) collective-permute-start(bf16[1,1536]{1,0:T(2,128)(2,1)} %bitcast.42), channel_id=1, source_target_pairs={{4,0},{8,4},{12,8},{5,1},{9,5},{13,9},{6,2},{10,6},{14,10},{7,3},{... | collective-permute-start | bytes 9224 | tf_op jit(solution)/shard_map/ppermute | solution.py:30
  145.5 29.3 %copy-start.9 = (f32[64,6]{0,1:T(8,128)S(1)}, f32[64,6]{0,1:T(8,128)}, u32[]{:S(2)}) copy-start(f32[64,6]{0,1:T(8,128)} %copy-done.8) | copy-start | bytes 4612
  149.0 74.3 %all-reduce.11.cloned.1.call-start = ((), (), s32[]{:S(2)}) async-start(), calls=%async_computation.3 | async-start | bytes 393216 | tf_op jit(solution)/shard_map/psum | solution.py:36
  173.0 5.5 %collective-permute-start.4 = (f32[64,6]{0,1:T(8,128)S(1)}, f32[64,6]{0,1:T(8,128)S(1)}, u32[]{:S(2)}, u32[]{:S(2)}) collective-permute-start(f32[64,6]{0,1:T(8,128)S(1)} %multiply_reduce_fusion), channel_id=1, source_target_pairs={{0,4},{4,8},{8,12},{12,0},{1,5},{5,9},{9,13},{13,1},{2,6},{6,10},{... | collective-permute-start | bytes 4616 | tf_op jit(solution)/shard_map/ppermute | solution.py:18
  176.9 25.3 %copy-start.2 = (bf16[64,1,6,64]{3,2,1,0:T(8,128)(2,1)S(1)}, bf16[64,1,6,64]{3,2,1,0:T(8,128)(2,1)}, u32[]{:S(2)}) copy-start(bf16[64,1,6,64]{3,2,1,0:T(8,128)(2,1)} %copy-done.1) | copy-start | bytes 147460
  178.4 18.1 %collective-permute-start.5 = (f32[64,6]{0,1:T(8,128)S(1)}, f32[64,6]{0,1:T(8,128)S(1)}, u32[]{:S(2)}, u32[]{:S(2)}) collective-permute-start(f32[64,6]{0,1:T(8,128)S(1)} %collective-permute-done.4), channel_id=1, source_target_pairs={{0,4},{4,8},{8,12},{12,0},{1,5},{5,9},{9,13},{13,1},{2,6},{6,10},{... | collective-permute-start | bytes 4616 | tf_op jit(solution)/shard_map/ppermute | solution.py:18
  196.6 5.5 %collective-permute-start.6 = (f32[64,6]{0,1:T(8,128)S(1)}, f32[64,6]{0,1:T(8,128)S(1)}, u32[]{:S(2)}, u32[]{:S(2)}) collective-permute-start(f32[64,6]{0,1:T(8,128)S(1)} %collective-permute-done.5), channel_id=1, source_target_pairs={{0,4},{4,8},{8,12},{12,0},{1,5},{5,9},{9,13},{13,1},{2,6},{6,10},{... | collective-permute-start | bytes 4616 | tf_op jit(solution)/shard_map/ppermute | solution.py:18
  203.2 20.0 %copy-start.4 = (f32[64,768]{1,0:T(8,128)S(1)}, f32[64,768]{1,0:T(8,128)}, u32[]{:S(2)}) copy-start(f32[64,768]{1,0:T(8,128)} %all-reduce.9.cloned.1.call-done) | copy-start | bytes 589828
Sparse Core Ops, SparseCore 0:
  52.5 18.4 all-reduce.4
  89.8 18.2 all-reduce.6
  149.1 19.4 all-reduce.8
  205.6 17.5 all-reduce.10
